TPU v7x, 512 devices: a whole 4x4x16 slice. The times are simulated.
512 devices in a mesh: row: 32 (over y, x, core), col: 16 (over z).
Axes of the slice: x: 4, y: 4, z: 16, core: 2. Of those that a mesh axis runs over, the one named last changes fastest.
Arguments:
- tokens: bfloat16 [4096, 6144], P('row', 'col'), may hold values from -6 to 6
- weight_blocks: bfloat16 [16, 128, 4096], P('col', 'row'), may hold values from -0.375 to 0.375
- block_rows: int32 [16, 128], P('col', 'row'), may hold values from 0 to 95, as said below
- block_columns: int32 [16, 128], P('col', 'row'), may hold values from 0 to 47
- panel_counts: int32 [16], P('col'), may hold values from 16 to 128, as said below
- hidden_grad: bfloat16 [4096, 49152], P('row', 'col'), may hold values from -1.1953125 to 1.1953125
Outputs:
- hidden: bfloat16 [4096, 49152], P('row', 'col')
- input_grad: bfloat16 [4096, 6144], P('row', 'col')
- weight_grad: bfloat16 [16, 128, 4096], P('col', 'row')
Inputs may be any that keep to these rules, and one draw needn't show every extreme that they name: `block_rows`: in each panel the live slots name distinct pairs of block row and block column; ids in the other slots lie in the same ranges and mean nothing. `panel_counts`: some panel has all 128 slots live.
All inputs are finite; a program needn't handle non-finite values.
Results may differ from a plain program's by a relative error of at most 0.02.
Values may be sent and summed in bfloat16 or wider, within the bound.
No kernel may reach another device: no remote copies, remote signals or barrier semaphores. Data moves between devices by JAX's collectives and lax.ppermute only.
A program may use at most 64 MiB of HBM per device.

v0:
```python
import math
import jax
import jax.numpy as jnp
from jax import lax
from jax.sharding import PartitionSpec as P

root_two_pi = 0.7978845608028654
cubic_term = 0.044715


def gelu_value(pre_act):
    inner = root_two_pi * (pre_act + cubic_term * pre_act * pre_act * pre_act)
    return 0.5 * pre_act * (1.0 + jnp.tanh(inner))


def gelu_slope(pre_act):
    inner = root_two_pi * (pre_act + cubic_term * pre_act * pre_act * pre_act)
    tangent = jnp.tanh(inner)
    return 0.5 * (1.0 + tangent) + 0.5 * pre_act * (1.0 - tangent * tangent) * root_two_pi * (
        1.0 + 3.0 * cubic_term * pre_act * pre_act
    )


def grouped_inputs(blocks, rows_here, cols_here, live_here):
    length = rows_here.shape[0]
    stride = max([width for width in range(1, 65) if length % width == 0])
    group_count = length // stride
    block_side = math.isqrt(blocks.shape[-1])
    shaped = blocks.reshape(group_count, stride, block_side, block_side)
    return (
        shaped,
        rows_here.reshape(group_count, stride),
        cols_here.reshape(group_count, stride),
        live_here.reshape(group_count, stride),
    )


def forward_blocks(running_start, token_blocks, blocks, rows_here, cols_here, live_here):
    tok_rows = token_blocks.shape[0]
    block_side = token_blocks.shape[2]

    def forward_advance(running, inputs):
        part_blocks, part_rows, part_cols, part_live = inputs
        masked = jnp.where(part_live[:, None, None], part_blocks, jnp.zeros_like(part_blocks))
        picked = jnp.take(token_blocks, part_rows, axis=1)
        products = jnp.einsum("tsa,sab->stb", picked, masked, preferred_element_type=jnp.float32)
        return (
            running.at[part_cols].add(products.reshape(part_rows.shape[0], tok_rows * block_side)),
            None,
        )

    result, unused = lax.scan(
        forward_advance, running_start, grouped_inputs(blocks, rows_here, cols_here, live_here)
    )
    return result


def backward_blocks(running_start, grad_blocks, blocks, rows_here, cols_here, live_here):
    tok_rows = grad_blocks.shape[0]
    block_side = grad_blocks.shape[2]

    def backward_advance(running, inputs):
        part_blocks, part_rows, part_cols, part_live = inputs
        masked = jnp.where(part_live[:, None, None], part_blocks, jnp.zeros_like(part_blocks))
        picked = jnp.take(grad_blocks, part_cols, axis=1)
        products = jnp.einsum("tsb,sab->sta", picked, masked, preferred_element_type=jnp.float32)
        return (
            running.at[part_rows].add(products.reshape(part_rows.shape[0], tok_rows * block_side)),
            None,
        )

    result, unused = lax.scan(
        backward_advance, running_start, grouped_inputs(blocks, rows_here, cols_here, live_here)
    )
    return result


def on_device(tokens, weight_blocks, block_rows, block_columns, panel_counts, hidden_grad):
    whole = lax.all_gather(tokens, "col", axis=1, tiled=True)
    tok_rows = whole.shape[0]
    block_side = math.isqrt(weight_blocks.shape[2])
    row_blocks = whole.shape[1] // block_side
    col_blocks = hidden_grad.shape[1] // block_side
    per_device = weight_blocks.shape[1]
    capacity = per_device * lax.axis_size("row")
    count_live = panel_counts[0]
    token_blocks = whole.reshape(tok_rows, row_blocks, block_side)
    empty_pre = jnp.zeros((col_blocks, tok_rows * block_side), jnp.float32)
    empty_ids = jnp.zeros((capacity,), jnp.int32)
    shard_piece = (
        lax.all_gather(weight_blocks, "row", axis=1, tiled=True),
        lax.all_gather(block_rows, "row", axis=1, tiled=True),
        lax.all_gather(block_columns, "row", axis=1, tiled=True),
    )
    begin_at = jnp.int32(0)
    pre_sum = empty_pre
    fold_rows_all = empty_ids
    fold_cols_all = empty_ids
    rows_here = shard_piece[1][0]
    cols_here = shard_piece[2][0]
    live_here = jnp.arange(rows_here.shape[0], dtype=jnp.int32) < count_live
    pre_sum = forward_blocks(
        pre_sum, token_blocks, shard_piece[0][0], rows_here, cols_here, live_here
    )
    fold_rows_all = lax.dynamic_update_slice_in_dim(fold_rows_all, rows_here, begin_at, 0)
    fold_cols_all = lax.dynamic_update_slice_in_dim(fold_cols_all, cols_here, begin_at, 0)
    pre_sum, rows_all, cols_all = (pre_sum, fold_rows_all, fold_cols_all)
    pre_act = pre_sum.reshape(col_blocks, tok_rows, block_side).transpose(1, 0, 2)
    hidden = gelu_value(pre_act).astype(jnp.bfloat16).reshape(tok_rows, col_blocks * block_side)
    upstream = hidden_grad.reshape(tok_rows, col_blocks, block_side)
    grad_blocks = (upstream.astype(jnp.float32) * gelu_slope(pre_act)).astype(jnp.bfloat16)
    empty_back = jnp.zeros((row_blocks, tok_rows * block_side), jnp.float32)
    shard_piece = (
        lax.all_gather(weight_blocks, "row", axis=1, tiled=True),
        lax.all_gather(block_rows, "row", axis=1, tiled=True),
        lax.all_gather(block_columns, "row", axis=1, tiled=True),
    )
    rows_here = shard_piece[1][0]
    cols_here = shard_piece[2][0]
    live_here = jnp.arange(rows_here.shape[0], dtype=jnp.int32) < count_live
    input_part = backward_blocks(
        empty_back, grad_blocks, shard_piece[0][0], rows_here, cols_here, live_here
    )
    own_sums = lax.psum_scatter(
        input_part.astype(jnp.bfloat16), "col", scatter_dimension=0, tiled=True
    ).astype(jnp.float32)
    input_grad = (
        own_sums.reshape(-1, tok_rows, block_side)
        .transpose(1, 0, 2)
        .reshape(tok_rows, -1)
        .astype(jnp.bfloat16)
    )
    live_part = jnp.arange(per_device * lax.axis_size("row"), dtype=jnp.int32) < count_live
    picked_in = jnp.take(token_blocks, rows_all, axis=1)
    picked_grad = jnp.take(grad_blocks, cols_all, axis=1)
    products = jnp.einsum(
        "tsa,tsb->sab", picked_in, picked_grad, preferred_element_type=jnp.float32
    )
    products = jnp.where(live_part[:, None, None], products, jnp.zeros_like(products))
    weight_sum = lax.psum_scatter(
        products.reshape(per_device * lax.axis_size("row"), block_side * block_side).astype(
            jnp.bfloat16
        ),
        "row",
        scatter_dimension=0,
        tiled=True,
    )
    weight_grad = weight_sum.reshape(1, per_device, block_side * block_side)
    return (hidden, input_grad, weight_grad)


def solution(mesh):
    placed = (
        P("row", "col"),
        P("col", "row", None),
        P("col", "row"),
        P("col", "row"),
        P("col"),
        P("row", "col"),
    )
    return jax.shard_map(
        on_device,
        mesh=mesh,
        in_specs=placed,
        out_specs=(P("row", "col"), P("row", "col"), P("col", "row", None)),
        check_vma=False,
    )
```

profile of v0, /device:TPU:1, one launch (start us, length us, event | category | flops | bytes accessed | tf_op | source)
XLA Modules:
  0.0 446.8 jit_solution(2087213582369064578)
XLA Ops:
  15.8 14.4 %all-reduce.5 = (s32[128]{0:T(128)S(1)}, s32[128]{0:T(128)S(1)}) all-reduce(s32[128]{0:T(128)S(1)} %bitcast_dynamic-update-slice_fusion.1, s32[128]{0:T(128)S(1)} %bitcast_dynamic-update-slice_fusion), channel_id=1, replica_groups=mesh['row'=32,'col'=16] {'row'}, use_global_device_ids=true, to_apply=%add | all-reduce | flops 256 | bytes 2048 | tf_op jit(solution)/shard_map/squeeze | solution.py:100
  35.5 41.1 %all-gather.5.cloned.1.call-done = bf16[1,128,4096]{2,0,1:T(2,128)(2,1)} async-done(((bf16[1,4,4096]{2,0,1:T(2,128)(2,1)}), bf16[1,128,4096]{2,0,1:T(2,128)(2,1)}) %all-gather.5.cloned.1.call-update) | async-done | bytes 1048592 | tf_op jit(solution)/shard_map/all_gather | solution.py:91
  76.6 7.7 %reduce = bf16[128,4096]{1,0:T(8,128)(2,1)S(1)} reduce(bf16[1,128,4096]{2,0,1:T(2,128)(2,1)} %all-gather.5.cloned.1.call-done, bf16[]{:T(256)} %constant.132), dimensions={0}, to_apply=%all_gather.18.reduce_sub_computation | reduce | bytes 2097154 | tf_op jit(solution)/shard_map/all_gather | solution.py:91
  84.3 3.5 reshape_squeeze.14
  87.8 53.0 %all-gather.3.cloned.1.call-done = bf16[128,6144]{0,1:T(8,128)(2,1)} async-done(((bf16[128,384]{0,1:T(8,128)(2,1)}), bf16[128,6144]{0,1:T(8,128)(2,1)}) %all-gather.3.cloned.1.call-update) | async-done | bytes 1572880 | tf_op jit(solution)/shard_map/all_gather | solution.py:79
  140.9 40.8 %while.20 = (s32[]{:T(128)}, f32[48,8192]{1,0:T(8,128)S(1)}, s32[2,64]{1,0:T(2,128)S(1)}, s32[2,64]{1,0:T(2,128)S(1)}, bf16[128,96,64]{0,2,1:T(8,128)(2,1)}, /*i...) while((s32[]{:T(128)}, f32[48,8192]{1,0:T(8,128)S(1)}, s32[2,64]{1,0:T(2,128)S(1)}, ...), condition=%wide.region_2.3_spmd, body=%wide.region_0.2_spmd.sunk | while | flops 68421376 | bytes 18356652 | solution.py:52
  147.8 4.1 fusion.54
  151.9 4.8 %reshape.324 = f32[64,8192]{1,0:T(8,128)} reshape(f32[64,128,64]{2,1,0:T(8,128)} %fusion.54) | data formatting | bytes 4194304 | tf_op jit(solution)/shard_map/while/body/eval_jaxpr/reshape | solution.py:48
  156.7 4.6 %scatter_fusion = f32[48,8192]{1,0:T(8,128)S(1)} fusion(f32[48,8192]{1,0:T(8,128)S(1)} %get-tuple-element.269, s32[64]{0:T(128)S(1)} %get-tuple-element.249, f32[64,8192]{1,0:T(8,128)} %reshape.324), kind=kCustom, calls=%fused_computation.4.clone.1 | custom fusion | flops 524288 | bytes 6291712 | tf_op jit(solution)/shard_map/while/body/eval_jaxpr/scatter-add | solution.py:48
  168.1 4.1 fusion.54
  172.2 4.8 %reshape.324 = f32[64,8192]{1,0:T(8,128)} reshape(f32[64,128,64]{2,1,0:T(8,128)} %fusion.54) | data formatting | bytes 4194304 | tf_op jit(solution)/shard_map/while/body/eval_jaxpr/reshape | solution.py:48
  177.1 4.6 %scatter_fusion = f32[48,8192]{1,0:T(8,128)S(1)} fusion(f32[48,8192]{1,0:T(8,128)S(1)} %get-tuple-element.269, s32[64]{0:T(128)S(1)} %get-tuple-element.249, f32[64,8192]{1,0:T(8,128)} %reshape.324), kind=kCustom, calls=%fused_computation.4.clone.1 | custom fusion | flops 524288 | bytes 6291712 | tf_op jit(solution)/shard_map/while/body/eval_jaxpr/scatter-add | solution.py:48
  181.7 2.4 reshape.237
  184.1 2.3 copy.55
  189.1 34.9 %while.21 = (s32[]{:T(128)}, f32[96,8192]{1,0:T(8,128)S(1)}, s32[2,64]{1,0:T(2,128)S(1)}, s32[2,64]{1,0:T(2,128)S(1)}, bf16[128,48,64]{0,2,1:T(8,128)(2,1)}, /*i...) while((s32[]{:T(128)}, f32[96,8192]{1,0:T(8,128)S(1)}, s32[2,64]{1,0:T(2,128)S(1)}, ...), condition=%wide.region_5.6_spmd, body=%wide.region_3.5_spmd.sunk | while | flops 68421376 | bytes 16783788 | solution.py:72
  189.4 2.8 gather_fusion.1
  192.2 4.4 fusion.57
  196.6 4.8 %reshape.329 = f32[64,8192]{1,0:T(8,128)} reshape(f32[64,128,64]{2,1,0:T(8,128)} %fusion.57) | data formatting | bytes 4194304 | tf_op jit(solution)/shard_map/while/body/eval_jaxpr/reshape | solution.py:68
  201.4 5.2 %scatter_fusion.1 = f32[96,8192]{1,0:T(8,128)S(1)} fusion(f32[96,8192]{1,0:T(8,128)S(1)} %get-tuple-element.293, s32[64]{0:T(128)S(1)} %get-tuple-element.258, f32[64,8192]{1,0:T(8,128)} %reshape.329), kind=kCustom, calls=%fused_computation.5.clone.1 | custom fusion | flops 524288 | bytes 6291712 | tf_op jit(solution)/shard_map/while/body/eval_jaxpr/scatter-add | solution.py:68
  206.7 2.8 gather_fusion.1
  209.5 4.4 fusion.57
  213.9 4.8 %reshape.329 = f32[64,8192]{1,0:T(8,128)} reshape(f32[64,128,64]{2,1,0:T(8,128)} %fusion.57) | data formatting | bytes 4194304 | tf_op jit(solution)/shard_map/while/body/eval_jaxpr/reshape | solution.py:68
  218.7 5.2 %scatter_fusion.1 = f32[96,8192]{1,0:T(8,128)S(1)} fusion(f32[96,8192]{1,0:T(8,128)S(1)} %get-tuple-element.293, s32[64]{0:T(128)S(1)} %get-tuple-element.258, f32[64,8192]{1,0:T(8,128)} %reshape.329), kind=kCustom, calls=%fused_computation.5.clone.1 | custom fusion | flops 524288 | bytes 6291712 | tf_op jit(solution)/shard_map/while/body/eval_jaxpr/scatter-add | solution.py:68
  225.3 33.0 %fusion = bf16[8,8192]{1,0:T(8,128)(2,1)S(1)} fusion(bf16[96,8192]{1,0:T(8,128)(2,1)} %convert_element_type.36), kind=kCustom, calls=%all-reduce-scatter | all-reduce-scatter fusion | flops 1048577 | bytes 1705984
  258.3 3.7 collective-permute-start.2
  261.9 4.3 collective-permute-start.1
  267.6 2.4 gather_fusion.3
  270.0 2.4 gather_fusion.2
  272.4 4.8 %fusion.27 = bf16[128,64,64]{2,1,0:T(8,128)(2,1)} fusion(bf16[128,128,64]{1,2,0:T(8,128)(2,1)} %gather_fusion.3, bf16[128,128,64]{1,2,0:T(8,128)(2,1)} %gather_fusion.2, pred[128]{0:T(512)(128)(4,1)S(1)} %copy-done.4, pred[128]{0:T(512)(128)(4,1)S(1)} %copy-done.5), kind=kOutput, calls=%fused_computation.53 | convolution fusion | flops 136314880 | bytes 5243136 | tf_op jit(solution)/shard_map/tsa,tsb->sab/dot_general | solution.py:136
  277.2 3.4 copy.58
  280.6 5.1 %collective-permute-start.3 = (bf16[6,8192]{1,0:T(8,128)(2,1)S(1)}, bf16[6,8192]{1,0:T(8,128)(2,1)S(1)}, u32[]{:S(2)}, u32[]{:S(2)}) collective-permute-start(bf16[6,8192]{1,0:T(8,128)(2,1)S(1)} %slice.8), channel_id=1, source_target_pairs={{0,4},{1,5},{2,6},{3,7},{4,8},{5,9},{6,10},{7,11},{8,12},{9,13},{1... | collective-permute-start | bytes 294920
  291.2 146.5 %all-reduce.8.cloned.1.call-done = bf16[128,4096]{0,1:T(8,128)(2,1)} async-done(((bf16[128,4096]{0,1:T(8,128)(2,1)}), bf16[128,4096]{0,1:T(8,128)(2,1)}) %all-reduce.8.cloned.1.call-update) | async-done | bytes 1048592
  (77 shorter events, 38.4 us)
Async XLA Ops:
  7.2 69.4 %all-gather.5.cloned.1.call-start = ((), (), s32[]{:S(2)}) async-start(), calls=%async_computation.1 | async-start | bytes 2162688 | tf_op jit(solution)/shard_map/all_gather | solution.py:91
  8.7 132.1 %all-gather.3.cloned.1.call-start = ((), (), s32[]{:S(2)}) async-start(), calls=%async_computation | async-start | bytes 1671168 | tf_op jit(solution)/shard_map/all_gather | solution.py:79
  10.4 427.3 %all-reduce.8.cloned.1.call-start = ((), (), s32[]{:S(2)}) async-start(), calls=%async_computation.2 | async-start | bytes 2097152
  225.3 42.3 %copy-start = (bf16[128,48,64]{0,2,1:T(8,128)(2,1)S(1)}, bf16[128,48,64]{0,2,1:T(8,128)(2,1)}, u32[]{:S(2)}) copy-start(bf16[128,48,64]{0,2,1:T(8,128)(2,1)} %get-tuple-element.311) | copy-start | bytes 2359300
  258.3 30.2 %collective-permute-start.2 = (bf16[8,8192]{1,0:T(8,128)(2,1)S(1)}, bf16[8,8192]{1,0:T(8,128)(2,1)S(1)}, u32[]{:S(2)}, u32[]{:S(2)}) collective-permute-start(bf16[8,8192]{1,0:T(8,128)(2,1)S(1)} %fusion), channel_id=1, source_target_pairs={{0,3},{1,4},{2,5},{3,6},{4,7},{5,8},{6,9},{7,10},{8,11},{9,12},{10... | collective-permute-start | bytes 393224
  261.9 26.6 %collective-permute-start.1 = (bf16[8,8192]{1,0:T(8,128)(2,1)S(1)}, bf16[8,8192]{1,0:T(8,128)(2,1)S(1)}, u32[]{:S(2)}, u32[]{:S(2)}) collective-permute-start(bf16[8,8192]{1,0:T(8,128)(2,1)S(1)} %fusion), channel_id=1, source_target_pairs={{0,2},{1,3},{2,4},{3,5},{4,6},{5,7},{6,8},{7,9},{8,10},{9,11},{10,... | collective-permute-start | bytes 393224
  266.2 22.2 %collective-permute-start = (bf16[8,8192]{1,0:T(8,128)(2,1)S(1)}, bf16[8,8192]{1,0:T(8,128)(2,1)S(1)}, u32[]{:S(2)}, u32[]{:S(2)}) collective-permute-start(bf16[8,8192]{1,0:T(8,128)(2,1)S(1)} %fusion), channel_id=1, source_target_pairs={{0,1},{1,2},{2,3},{3,4},{4,5},{5,6},{6,7},{7,8},{8,9},{9,10},{10,1... | collective-permute-start | bytes 393224
  267.5 2.4 copy-start.1
  270.0 2.4 copy-start.4
  270.0 2.4 copy-start.5
  277.2 8.5 %copy-start.3 = (pred[128]{0:T(512)(128)(4,1)S(1)}, pred[128]{0:T(512)(128)(4,1)}, u32[]{:S(2)}) copy-start(pred[128]{0:T(512)(128)(4,1)} %iota_compare_fusion) | copy-start | bytes 388
  277.2 9.8 %copy-start.2 = (bf16[128,48,64]{0,2,1:T(8,128)(2,1)S(1)}, bf16[128,48,64]{0,2,1:T(8,128)(2,1)}, u32[]{:S(2)}) copy-start(bf16[128,48,64]{0,2,1:T(8,128)(2,1)} %get-tuple-element.161) | copy-start | bytes 2359300
  280.6 7.9 %collective-permute-start.3 = (bf16[6,8192]{1,0:T(8,128)(2,1)S(1)}, bf16[6,8192]{1,0:T(8,128)(2,1)S(1)}, u32[]{:S(2)}, u32[]{:S(2)}) collective-permute-start(bf16[6,8192]{1,0:T(8,128)(2,1)S(1)} %slice.8), channel_id=1, source_target_pairs={{0,4},{1,5},{2,6},{3,7},{4,8},{5,9},{6,10},{7,11},{8,12},{9,13},{1... | collective-permute-start | bytes 294920
Sparse Core Ops, SparseCore 0:
  11.7 64.8 all-gather.4
  79.3 61.5 all-gather.2
  288.3 149.3 all-reduce.7
where the time goes:
time: 448 us; the launch traced here: 447 us
  waiting for transfers between devices  241 us (54%)
  local copies, waits for them, and re-layouts  70.5 us (16%)
  blocking collectives  47.4 us (11%)
  other arithmetic  34.7 us (8%)
  matrix products  21.9 us (5%)
  between operations  16.4 us (4%)
  starting transfers between devices  14.4 us (3%)
    unnamed x8, waiting for transfers between devices  147 us
    all_gather x1, waiting for transfers between devices, on_device(): whole = lax.all_gather(tokens, 'col', axis=1, tiled=True)  53 us
    all_gather x1, waiting for transfers between devices, on_device(): lax.all_gather(weight_blocks, 'row', axis=1, tiled=True)  41.1 us
    unnamed x1, blocking collectives  33 us
    squeeze x1, blocking collectives, on_device(): cols_here = shard_piece[2][0]  14.4 us
    unnamed x5, starting transfers between devices  14.4 us
    unnamed x27, local copies, waits for them, and re-layouts  13.3 us
    scatter-add x2, other arithmetic, backward_advance(): running.at[part_rows]  10.4 us
  transfers between devices with their start and end apart: 7, of which 4 were waited for; matrix products, arithmetic and copies ran while one was open for 9% of the time, Pallas kernels for 0%

commit v1 on v0

--- a/solution.py
+++ b/solution.py
@@ -6,6 +6,23 @@
 
 root_two_pi = 0.7978845608028654
 cubic_term = 0.044715
+
+
+def laid_out(blocks, dim):
+    lengths = list(blocks.shape[1:])
+    lengths[dim] *= blocks.shape[0]
+    return jnp.moveaxis(blocks, 0, dim).reshape(lengths)
+
+
+def collected_by_bits(shard, axis):
+    size, here = (lax.axis_size(axis), lax.axis_index(axis))
+    pieces, stride = (shard[None], 1)
+    while stride < size:
+        other = lax.ppermute(pieces, axis, [(i, i ^ stride) for i in range(size)])
+        low = here & stride == 0
+        pieces = jnp.concatenate([jnp.where(low, pieces, other), jnp.where(low, other, pieces)])
+        stride *= 2
+    return pieces
 
 
 def gelu_value(pre_act):
@@ -76,7 +93,7 @@
 
 
 def on_device(tokens, weight_blocks, block_rows, block_columns, panel_counts, hidden_grad):
-    whole = lax.all_gather(tokens, "col", axis=1, tiled=True)
+    whole = laid_out(collected_by_bits(tokens, "col"), 1)
     tok_rows = whole.shape[0]
     block_side = math.isqrt(weight_blocks.shape[2])
     row_blocks = whole.shape[1] // block_side

time: 448 us -> 462 us (1.031)
  starting transfers between devices: 14.4 us -> 66.2 us
  waiting for transfers between devices: 241 us -> 191 us
  blocking collectives: 47.4 us -> 61.1 us
    all_gather x1 -> x0, waiting for transfers between devices: 53 us -> none  [on_device(): whole = lax.all_gather(tokens, 'col', axis=1, tiled=True)]
    ppermute x0 -> x4, waiting for transfers between devices: none -> 52.1 us  [collected_by_bits(): other = lax.ppermute(pieces, axis, [(i, i ^ stride) for i in range(size)])]
    ppermute x0 -> x4, starting transfers between devices: none -> 51.7 us  [collected_by_bits(): other = lax.ppermute(pieces, axis, [(i, i ^ stride) for i in range(size)])]
    all_gather x1, waiting for transfers between devices: 41.1 us -> 0.01 us  [on_device(): lax.all_gather(weight_blocks, 'row', axis=1, tiled=True)]
    unnamed x1, blocking collectives: 33 us -> 45.7 us
    unnamed x8 -> x7, waiting for transfers between devices: 147 us -> 139 us
    unnamed x27 -> x35, local copies, waits for them, and re-layouts: 13.3 us -> 10.3 us
  transfers between devices with their start and end apart: 7 -> 10, of which waited for: 4 -> 5; matrix products, arithmetic and copies ran while one was open for 9% -> 6% of each run, Pallas kernels for 0% -> 0%
where the time goes in v1:
time: 462 us; the launch traced here: 461 us
  waiting for transfers between devices  191 us (41%)
  local copies, waits for them, and re-layouts  67.2 us (15%)
  starting transfers between devices  66.2 us (14%)
  blocking collectives  61.1 us (13%)
  other arithmetic  36.7 us (8%)
  matrix products  21.3 us (5%)
  between operations  17 us (4%)
    unnamed x7, waiting for transfers between devices  139 us
    ppermute x4, waiting for transfers between devices, collected_by_bits(): other = lax.ppermute(pieces, axis, [(i, i ^ stride) for i in range(size)])  52.1 us
    ppermute x4, starting transfers between devices, collected_by_bits(): other = lax.ppermute(pieces, axis, [(i, i ^ stride) for i in range(size)])  51.7 us
    unnamed x1, blocking collectives  45.7 us
    squeeze x1, blocking collectives, on_device(): cols_here = shard_piece[2][0]  15.4 us
    unnamed x5, starting transfers between devices  14.5 us
    scatter-add x2, other arithmetic, backward_advance(): running.at[part_rows]  10.4 us
    unnamed x35, local copies, waits for them, and re-layouts  10.3 us
  transfers between devices with their start and end apart: 10, of which 5 were waited for; matrix products, arithmetic and copies ran while one was open for 6% of the time, Pallas kernels for 0%

profile of v1, /device:TPU:1, one launch (start us, length us, event | category | flops | bytes accessed | tf_op | source)
XLA Modules:
  0.0 460.9 jit_solution(3070707590614838483)
XLA Ops:
  8.2 4.4 collective-permute-start
  14.7 5.3 %collective-permute-start.1 = (bf16[2,128,384]{1,2,0:T(8,128)(2,1)S(1)}, bf16[2,128,384]{1,2,0:T(8,128)(2,1)S(1)}, u32[]{:S(2)}, u32[]{:S(2)}) collective-permute-start(bf16[2,128,384]{1,2,0:T(8,128)(2,1)S(1)} %pad_maximum_fusion.3), channel_id=1, source_target_pairs={{0,2},{1,3},{2,0},{3,1},{4,6},{5,7},{6,4},{7,5},{8,10},{9,11},{10,... | collective-permute-start | bytes 589832 | tf_op jit(solution)/shard_map/ppermute | solution.py:21
  25.2 12.5 %collective-permute-start.2 = (bf16[4,128,384]{1,2,0:T(8,128)(2,1)S(1)}, bf16[4,128,384]{1,2,0:T(8,128)(2,1)S(1)}, u32[]{:S(2)}, u32[]{:S(2)}) collective-permute-start(bf16[4,128,384]{1,2,0:T(8,128)(2,1)S(1)} %pad_maximum_fusion.2), channel_id=1, source_target_pairs={{0,4},{1,5},{2,6},{3,7},{4,0},{5,1},{6,2},{7,3},{8,12},{9,13},{10,... | collective-permute-start | bytes 1179656 | tf_op jit(solution)/shard_map/ppermute | solution.py:21
  38.7 32.9 %collective-permute-done.2 = bf16[4,128,384]{1,2,0:T(8,128)(2,1)S(1)} collective-permute-done((bf16[4,128,384]{1,2,0:T(8,128)(2,1)S(1)}, bf16[4,128,384]{1,2,0:T(8,128)(2,1)S(1)}, u32[]{:S(2)}, u32[]{:S(2)}) %collective-permute-start.2) | collective-permute-done | bytes 393248 | tf_op jit(solution)/shard_map/ppermute | solution.py:21
  72.6 29.5 %collective-permute-start.3 = (bf16[8,128,384]{1,2,0:T(8,128)(2,1)}, bf16[8,128,384]{1,2,0:T(8,128)(2,1)}, u32[]{:S(2)}, u32[]{:S(2)}) collective-permute-start(bf16[8,128,384]{1,2,0:T(8,128)(2,1)} %pad_maximum_fusion.1), channel_id=1, source_target_pairs={{0,8},{1,9},{2,10},{3,11},{4,12},{5,13},{6,14},{7,15},{8,0},{9,1},... | collective-permute-start | bytes 2359304 | tf_op jit(solution)/shard_map/ppermute | solution.py:21
  103.4 15.4 %all-reduce.5 = (s32[128]{0:T(128)S(1)}, s32[128]{0:T(128)S(1)}) all-reduce(s32[128]{0:T(128)S(1)} %bitcast_dynamic-update-slice_fusion.1, s32[128]{0:T(128)S(1)} %bitcast_dynamic-update-slice_fusion), channel_id=1, replica_groups=mesh['row'=32,'col'=16] {'row'}, use_global_device_ids=true, to_apply=%add | all-reduce | flops 256 | bytes 2048 | tf_op jit(solution)/shard_map/squeeze | solution.py:117
  122.3 15.6 %collective-permute-done.3 = bf16[8,128,384]{1,2,0:T(8,128)(2,1)} collective-permute-done((bf16[8,128,384]{1,2,0:T(8,128)(2,1)}, bf16[8,128,384]{1,2,0:T(8,128)(2,1)}, u32[]{:S(2)}, u32[]{:S(2)}) %collective-permute-start.3) | collective-permute-done | bytes 786464 | tf_op jit(solution)/shard_map/ppermute | solution.py:21
  141.5 7.7 %reduce = bf16[128,4096]{1,0:T(8,128)(2,1)S(1)} reduce(bf16[1,128,4096]{2,0,1:T(2,128)(2,1)} %all-gather.2.cloned.1.call-done, bf16[]{:T(256)} %constant.144), dimensions={0}, to_apply=%all_gather.14.reduce_sub_computation | reduce | bytes 2097154 | tf_op jit(solution)/shard_map/all_gather | solution.py:108
  149.2 3.5 reshape_squeeze.14
  152.8 40.7 %while.20 = (s32[]{:T(128)}, f32[48,8192]{1,0:T(8,128)S(1)}, s32[2,64]{1,0:T(2,128)S(1)}, s32[2,64]{1,0:T(2,128)S(1)}, bf16[128,96,64]{0,2,1:T(8,128)(2,1)}, /*i...) while((s32[]{:T(128)}, f32[48,8192]{1,0:T(8,128)S(1)}, s32[2,64]{1,0:T(2,128)S(1)}, ...), condition=%wide.region_2.3_spmd, body=%wide.region_0.2_spmd.sunk | while | flops 68421376 | bytes 18356652 | solution.py:69
  159.7 4.1 fusion.54
  163.8 4.8 %reshape.320 = f32[64,8192]{1,0:T(8,128)} reshape(f32[64,128,64]{2,1,0:T(8,128)} %fusion.54) | data formatting | bytes 4194304 | tf_op jit(solution)/shard_map/while/body/eval_jaxpr/reshape | solution.py:65
  168.6 4.6 %scatter_fusion = f32[48,8192]{1,0:T(8,128)S(1)} fusion(f32[48,8192]{1,0:T(8,128)S(1)} %get-tuple-element.279, s32[64]{0:T(128)S(1)} %get-tuple-element.259, f32[64,8192]{1,0:T(8,128)} %reshape.320), kind=kCustom, calls=%fused_computation.4.clone.1 | custom fusion | flops 524288 | bytes 6291712 | tf_op jit(solution)/shard_map/while/body/eval_jaxpr/scatter-add | solution.py:65
  180.1 4.1 fusion.54
  184.2 4.8 %reshape.320 = f32[64,8192]{1,0:T(8,128)} reshape(f32[64,128,64]{2,1,0:T(8,128)} %fusion.54) | data formatting | bytes 4194304 | tf_op jit(solution)/shard_map/while/body/eval_jaxpr/reshape | solution.py:65
  189.0 4.6 %scatter_fusion = f32[48,8192]{1,0:T(8,128)S(1)} fusion(f32[48,8192]{1,0:T(8,128)S(1)} %get-tuple-element.279, s32[64]{0:T(128)S(1)} %get-tuple-element.259, f32[64,8192]{1,0:T(8,128)} %reshape.320), kind=kCustom, calls=%fused_computation.4.clone.1 | custom fusion | flops 524288 | bytes 6291712 | tf_op jit(solution)/shard_map/while/body/eval_jaxpr/scatter-add | solution.py:65
  201.0 34.9 %while.21 = (s32[]{:T(128)}, f32[96,8192]{1,0:T(8,128)S(1)}, s32[2,64]{1,0:T(2,128)S(1)}, s32[2,64]{1,0:T(2,128)S(1)}, bf16[128,48,64]{0,2,1:T(8,128)(2,1)}, /*i...) while((s32[]{:T(128)}, f32[96,8192]{1,0:T(8,128)S(1)}, s32[2,64]{1,0:T(2,128)S(1)}, ...), condition=%wide.region_5.6_spmd, body=%wide.region_3.5_spmd.sunk | while | flops 68421376 | bytes 16783788 | solution.py:89
  201.3 2.9 gather_fusion.1
  204.1 4.4 fusion.57
  208.6 4.8 %reshape.325 = f32[64,8192]{1,0:T(8,128)} reshape(f32[64,128,64]{2,1,0:T(8,128)} %fusion.57) | data formatting | bytes 4194304 | tf_op jit(solution)/shard_map/while/body/eval_jaxpr/reshape | solution.py:85
  213.3 5.2 %scatter_fusion.1 = f32[96,8192]{1,0:T(8,128)S(1)} fusion(f32[96,8192]{1,0:T(8,128)S(1)} %get-tuple-element.303, s32[64]{0:T(128)S(1)} %get-tuple-element.268, f32[64,8192]{1,0:T(8,128)} %reshape.325), kind=kCustom, calls=%fused_computation.5.clone.1 | custom fusion | flops 524288 | bytes 6291712 | tf_op jit(solution)/shard_map/while/body/eval_jaxpr/scatter-add | solution.py:85
  218.6 2.9 gather_fusion.1
  221.5 4.4 fusion.57
  225.9 4.8 %reshape.325 = f32[64,8192]{1,0:T(8,128)} reshape(f32[64,128,64]{2,1,0:T(8,128)} %fusion.57) | data formatting | bytes 4194304 | tf_op jit(solution)/shard_map/while/body/eval_jaxpr/reshape | solution.py:85
  230.7 5.2 %scatter_fusion.1 = f32[96,8192]{1,0:T(8,128)S(1)} fusion(f32[96,8192]{1,0:T(8,128)S(1)} %get-tuple-element.303, s32[64]{0:T(128)S(1)} %get-tuple-element.268, f32[64,8192]{1,0:T(8,128)} %reshape.325), kind=kCustom, calls=%fused_computation.5.clone.1 | custom fusion | flops 524288 | bytes 6291712 | tf_op jit(solution)/shard_map/while/body/eval_jaxpr/scatter-add | solution.py:85
  237.3 45.7 %fusion = bf16[8,8192]{1,0:T(8,128)(2,1)S(1)} fusion(bf16[96,8192]{1,0:T(8,128)(2,1)} %convert_element_type.36), kind=kCustom, calls=%all-reduce-scatter | all-reduce-scatter fusion | flops 1048577 | bytes 1705984
  284.5 3.2 collective-permute-start.5
  287.7 3.3 collective-permute-start.4
  293.3 4.2 fusion.27
  297.5 3.4 copy.59
  300.9 6.5 %collective-permute-start.7 = (bf16[6,8192]{1,0:T(8,128)(2,1)S(1)}, bf16[6,8192]{1,0:T(8,128)(2,1)S(1)}, u32[]{:S(2)}, u32[]{:S(2)}) collective-permute-start(bf16[6,8192]{1,0:T(8,128)(2,1)S(1)} %slice.8), channel_id=1, source_target_pairs={{0,4},{1,5},{2,6},{3,7},{4,8},{5,9},{6,10},{7,11},{8,12},{9,13},{1... | collective-permute-start | bytes 294920
  312.7 138.8 %all-reduce.8.cloned.1.call-done = bf16[128,4096]{0,1:T(8,128)(2,1)} async-done(((bf16[128,4096]{0,1:T(8,128)(2,1)}), bf16[128,4096]{0,1:T(8,128)(2,1)}) %all-reduce.8.cloned.1.call-update) | async-done | bytes 1048592
  (97 shorter events, 49.9 us)
Async XLA Ops:
  7.2 30.6 %copy-start.8 = (s32[1,4]{1,0:T(1,128)S(1)}, s32[1,4]{1,0:T(1,128)}, u32[]{:S(2)}) copy-start(s32[1,4]{1,0:T(1,128)} %param.12) | copy-start | bytes 52
  7.2 31.4 %copy-start.9 = (s32[1,4]{1,0:T(1,128)S(1)}, s32[1,4]{1,0:T(1,128)}, u32[]{:S(2)}) copy-start(s32[1,4]{1,0:T(1,128)} %param.13) | copy-start | bytes 52
  7.2 134.3 %all-gather.2.cloned.1.call-start = ((), (), s32[]{:S(2)}) async-start(), calls=%async_computation | async-start | bytes 2162688 | tf_op jit(solution)/shard_map/all_gather | solution.py:108
  8.2 6.4 %collective-permute-start = (bf16[1,128,384]{1,2,0:T(8,128)(2,1)S(1)}, bf16[1,128,384]{1,2,0:T(8,128)(2,1)S(1)}, u32[]{:S(2)}, u32[]{:S(2)}) collective-permute-start(bf16[1,128,384]{1,2,0:T(8,128)(2,1)S(1)} %bitcast.128), channel_id=1, source_target_pairs={{0,1},{1,0},{2,3},{3,2},{4,5},{5,4},{6,7},{7,6},{8,9},{9,8},{10,11... | collective-permute-start | bytes 294920 | tf_op jit(solution)/shard_map/ppermute | solution.py:21
  14.7 10.5 %collective-permute-start.1 = (bf16[2,128,384]{1,2,0:T(8,128)(2,1)S(1)}, bf16[2,128,384]{1,2,0:T(8,128)(2,1)S(1)}, u32[]{:S(2)}, u32[]{:S(2)}) collective-permute-start(bf16[2,128,384]{1,2,0:T(8,128)(2,1)S(1)} %pad_maximum_fusion.3), channel_id=1, source_target_pairs={{0,2},{1,3},{2,0},{3,1},{4,6},{5,7},{6,4},{7,5},{8,10},{9,11},{10,... | collective-permute-start | bytes 589832 | tf_op jit(solution)/shard_map/ppermute | solution.py:21
  21.4 430.0 %all-reduce.8.cloned.1.call-start = ((), (), s32[]{:S(2)}) async-start(), calls=%async_computation.1 | async-start | bytes 2097152
  25.2 93.8 %copy-start.4 = (bf16[128,3072]{1,0:T(8,128)(2,1)S(1)}, bf16[128,3072]{1,0:T(8,128)(2,1)}, u32[]{:S(2)}) copy-start(bf16[128,3072]{1,0:T(8,128)(2,1)} %param.15) | copy-start | bytes 2359300
  25.2 46.4 %collective-permute-start.2 = (bf16[4,128,384]{1,2,0:T(8,128)(2,1)S(1)}, bf16[4,128,384]{1,2,0:T(8,128)(2,1)S(1)}, u32[]{:S(2)}, u32[]{:S(2)}) collective-permute-start(bf16[4,128,384]{1,2,0:T(8,128)(2,1)S(1)} %pad_maximum_fusion.2), channel_id=1, source_target_pairs={{0,4},{1,5},{2,6},{3,7},{4,0},{5,1},{6,2},{7,3},{8,12},{9,13},{10,... | collective-permute-start | bytes 1179656 | tf_op jit(solution)/shard_map/ppermute | solution.py:21
  72.6 65.3 %collective-permute-start.3 = (bf16[8,128,384]{1,2,0:T(8,128)(2,1)}, bf16[8,128,384]{1,2,0:T(8,128)(2,1)}, u32[]{:S(2)}, u32[]{:S(2)}) collective-permute-start(bf16[8,128,384]{1,2,0:T(8,128)(2,1)} %pad_maximum_fusion.1), channel_id=1, source_target_pairs={{0,8},{1,9},{2,10},{3,11},{4,12},{5,13},{6,14},{7,15},{8,0},{9,1},... | collective-permute-start | bytes 2359304 | tf_op jit(solution)/shard_map/ppermute | solution.py:21
  139.3 2.2 copy-start.1
  237.3 53.7 %copy-start = (bf16[128,48,64]{0,2,1:T(8,128)(2,1)S(1)}, bf16[128,48,64]{0,2,1:T(8,128)(2,1)}, u32[]{:S(2)}) copy-start(bf16[128,48,64]{0,2,1:T(8,128)(2,1)} %get-tuple-element.320) | copy-start | bytes 2359300
  283.0 10.3 %copy-start.2 = (bf16[128,128,64]{1,2,0:T(8,128)(2,1)S(1)}, bf16[128,128,64]{1,2,0:T(8,128)(2,1)}, u32[]{:S(2)}) copy-start(bf16[128,128,64]{1,2,0:T(8,128)(2,1)} %gather_fusion.2) | copy-start | bytes 6291460
  283.0 10.2 %copy-start.6 = (pred[128]{0:T(512)(128)(4,1)S(1)}, pred[128]{0:T(512)(128)(4,1)}, u32[]{:S(2)}) copy-start(pred[128]{0:T(512)(128)(4,1)} %get-tuple-element.172) | copy-start | bytes 388
  283.1 10.2 %copy-start.7 = (pred[128]{0:T(512)(128)(4,1)S(1)}, pred[128]{0:T(512)(128)(4,1)}, u32[]{:S(2)}) copy-start(pred[128]{0:T(512)(128)(4,1)} %get-tuple-element.173) | copy-start | bytes 388
  283.1 26.9 %collective-permute-start.6 = (bf16[8,8192]{1,0:T(8,128)(2,1)S(1)}, bf16[8,8192]{1,0:T(8,128)(2,1)S(1)}, u32[]{:S(2)}, u32[]{:S(2)}) collective-permute-start(bf16[8,8192]{1,0:T(8,128)(2,1)S(1)} %fusion), channel_id=1, source_target_pairs={{0,3},{1,4},{2,5},{3,6},{4,7},{5,8},{6,9},{7,10},{8,11},{9,12},{10... | collective-permute-start | bytes 393224
  284.5 25.4 %collective-permute-start.5 = (bf16[8,8192]{1,0:T(8,128)(2,1)S(1)}, bf16[8,8192]{1,0:T(8,128)(2,1)S(1)}, u32[]{:S(2)}, u32[]{:S(2)}) collective-permute-start(bf16[8,8192]{1,0:T(8,128)(2,1)S(1)} %fusion), channel_id=1, source_target_pairs={{0,2},{1,3},{2,4},{3,5},{4,6},{5,7},{6,8},{7,9},{8,10},{9,11},{10,... | collective-permute-start | bytes 393224
  287.7 22.2 %collective-permute-start.4 = (bf16[8,8192]{1,0:T(8,128)(2,1)S(1)}, bf16[8,8192]{1,0:T(8,128)(2,1)S(1)}, u32[]{:S(2)}, u32[]{:S(2)}) collective-permute-start(bf16[8,8192]{1,0:T(8,128)(2,1)S(1)} %fusion), channel_id=1, source_target_pairs={{0,1},{1,2},{2,3},{3,4},{4,5},{5,6},{6,7},{7,8},{8,9},{9,10},{10,1... | collective-permute-start | bytes 393224
  297.5 9.9 %copy-start.5 = (pred[128]{0:T(512)(128)(4,1)S(1)}, pred[128]{0:T(512)(128)(4,1)}, u32[]{:S(2)}) copy-start(pred[128]{0:T(512)(128)(4,1)} %iota_compare_fusion) | copy-start | bytes 388
  297.5 11.2 %copy-start.3 = (bf16[128,48,64]{0,2,1:T(8,128)(2,1)S(1)}, bf16[128,48,64]{0,2,1:T(8,128)(2,1)}, u32[]{:S(2)}) copy-start(bf16[128,48,64]{0,2,1:T(8,128)(2,1)} %get-tuple-element.161) | copy-start | bytes 2359300
  300.9 9.0 %collective-permute-start.7 = (bf16[6,8192]{1,0:T(8,128)(2,1)S(1)}, bf16[6,8192]{1,0:T(8,128)(2,1)S(1)}, u32[]{:S(2)}, u32[]{:S(2)}) collective-permute-start(bf16[6,8192]{1,0:T(8,128)(2,1)S(1)} %slice.8), channel_id=1, source_target_pairs={{0,4},{1,5},{2,6},{3,7},{4,8},{5,9},{6,10},{7,11},{8,12},{9,13},{1... | collective-permute-start | bytes 294920
Sparse Core Ops, SparseCore 0:
  21.6 63.0 all-gather.1
  310.0 141.3 all-reduce.7
